TPU v7x, 32 devices: a whole 2x2x4 slice. The times are simulated.
32 devices in a mesh: member: 2 (over x), mesh: 8 (over z, y), writer: 2 (over core).
Axes of the slice: x: 2, y: 2, z: 4, core: 2. Of those that a mesh axis runs over, the one named last changes fastest.
Arguments:
- mesh_nodes: bfloat16 [16384, 512], P(('member', 'mesh'), 'writer'), parts along dimension 0, may hold values from -6 to 6
- grid_state: bfloat16 [80, 131072], P(None, ('member', 'mesh', 'writer')), parts along dimension 1, may hold values from -6 to 6
- interp: bfloat16 [512, 4, 128, 128], P('mesh'), may hold values from -0.25 to 0.25
- wanted: int32 [8, 32], P('mesh'), may hold values from 0 to 63, as said below
- tile_slots: int32 [512, 4], P('mesh'), may hold values from 0 to 31
- edge_count: int32 [512], P('mesh'), may hold values from 1 to 4
- w_in: bfloat16 [512, 512], replicated, may hold values from -0.25 to 0.25
- b_in: bfloat16 [512], replicated, may hold values from -4 to 4
- w_out: bfloat16 [512, 80], replicated, may hold values from -0.25 to 0.25
- b_out: bfloat16 [80], replicated, may hold values from -2 to 2
- writer_order: int32 [80], replicated, may hold values from 0 to 79, each once
Outputs:
- written: bfloat16 [80, 131072], P('writer', ('member', 'mesh')), parts along dimension 1
There are 2 independent parts, one for each index of `member`. A program takes and returns all parts, laid end to end along the dimension named above; an argument that names none is the same for every part. Nothing has to cross between parts.
Inputs may be any that keep to these rules, and one draw needn't show every extreme that they name: `wanted`: each row lists 32 different node blocks; at most 8 of them lie among the 8 blocks of one index of mesh, and exactly 8 do for one index, in every row.
All inputs are finite; a program needn't handle non-finite values.
Results may differ from a plain program's by a relative error of at most 0.0039.
Values may be sent and summed in bfloat16 or wider, within the bound.
No kernel may reach another device: no remote copies, remote signals or barrier semaphores. Data moves between devices by JAX's collectives and lax.ppermute only.
A program may use at most 128 MiB of HBM per device.

v0:
```python
import jax
import jax.numpy as jnp
from jax import lax
from jax.sharding import PartitionSpec as P

BLK = 128
K = 4


def local(
    mesh_nodes,
    grid_state,
    interp,
    wanted,
    tile_slots,
    edge_count,
    w_in,
    b_in,
    w_out,
    b_out,
    writer_order,
):
    half_width = mesh_nodes.shape[1]
    block_count = mesh_nodes.shape[0] // BLK
    own_blocks = mesh_nodes.reshape(block_count, BLK, half_width)
    block_ids = wanted[0]
    wanted_count = block_ids.shape[0]
    empty = jnp.zeros((wanted_count, BLK, half_width), jnp.bfloat16)
    block_piece = lax.all_gather(own_blocks, "mesh", axis=0, tiled=True)
    first_row = jnp.int32(0)
    piece_count = block_piece.shape[0]
    inside = (block_ids >= first_row) & (block_ids < first_row + piece_count)
    offset_ids = jnp.clip(block_ids, 0, piece_count - 1)
    picked = block_piece[offset_ids]
    fetched = jnp.where(inside[:, None, None], picked, empty)
    tile_count = interp.shape[0]
    summed = jnp.zeros((tile_count, BLK, half_width), jnp.float32)
    for slot_col in range(K):
        chosen = fetched[tile_slots[:, slot_col]]
        product = jnp.einsum(
            "tpn,tnf->tpf", interp[:, slot_col], chosen, preferred_element_type=jnp.float32
        )
        live_mask = (slot_col < edge_count)[:, None, None]
        summed = summed + jnp.where(live_mask, product, jnp.float32(0.0))
    aggregated = summed.reshape(tile_count * BLK, half_width).astype(jnp.bfloat16)
    weight_rows = lax.dynamic_slice_in_dim(
        w_in, lax.axis_index("writer") * half_width, half_width, 0
    )
    layer_one = lax.psum_scatter(
        jnp.dot(aggregated, weight_rows, preferred_element_type=jnp.float32),
        "writer",
        scatter_dimension=0,
        tiled=True,
    )
    hidden = jax.nn.silu(layer_one + b_in.astype(jnp.float32)).astype(jnp.bfloat16)
    decoded = lax.dot_general(
        w_out, hidden, (((0,), (1,)), ((), ())), preferred_element_type=jnp.float32
    )
    decoded = decoded + b_out.astype(jnp.float32)[:, None]
    combined = grid_state.astype(jnp.float32) + decoded
    ordered = combined[writer_order].astype(jnp.bfloat16)
    return lax.all_to_all(ordered, "writer", split_axis=0, concat_axis=1, tiled=True)


def solution(mesh):
    placed = (
        P(("member", "mesh"), "writer"),
        P(None, ("member", "mesh", "writer")),
        P("mesh", None, None, None),
        P("mesh", None),
        P("mesh", None),
        P("mesh"),
        P(),
        P(),
        P(),
        P(),
        P(),
    )
    return jax.shard_map(
        local,
        mesh=mesh,
        in_specs=placed,
        out_specs=P("writer", ("member", "mesh")),
        check_vma=False,
    )
```

profile of v0, /device:TPU:0, one launch (start us, length us, event | category | flops | bytes accessed | tf_op | source)
XLA Modules:
  0.0 187.7 jit_solution(383375123895336433)
XLA Ops:
  6.5 0.0 copy-start
  6.5 0.0 all-gather.2.cloned.1.call-start
  6.5 0.7 all-gather.2.cloned.1.call-update
  7.3 0.0 reduce-scatter.2.cloned.1.call-start
  7.3 0.7 fusion.15
  8.0 0.8 fusion.19
  8.8 0.7 and_bitcast_fusion
  9.5 0.7 broadcast_compare_fusion.3
  10.2 75.5 %all-gather.2.cloned.1.call-done = bf16[64,128,256]{2,1,0:T(8,128)(2,1)} async-done(((bf16[8,128,256]{2,1,0:T(8,128)(2,1)}), bf16[64,128,256]{2,1,0:T(8,128)(2,1)}) %all-gather.2.cloned.1.call-update) | async-done | bytes 4194320 | tf_op jit(solution)/shard_map/all_gather | solution.py:29
  85.6 4.2 %gather_fusion = bf16[32,128,256]{2,1,0:T(8,128)(2,1)} fusion(bf16[64,128,256]{2,1,0:T(8,128)(2,1)} %all-gather.2.cloned.1.call-done, s32[1024]{0:T(1024)S(1)} %pad_clamp_fusion.5), kind=kCustom, calls=%fused_computation | custom fusion | bytes 4194432 | tf_op jit(solution)/shard_map/gather | solution.py:34
  89.8 1.8 broadcast_select_fusion
  91.6 2.8 %gather_fusion.2 = bf16[64,128,256]{2,1,0:T(8,128)(2,1)} fusion(bf16[32,128,256]{2,1,0:T(8,128)(2,1)S(1)} %broadcast_select_fusion, s32[1024]{0:T(1024)S(1)} %get-tuple-element.15), kind=kCustom, calls=%fused_computation.2 | custom fusion | bytes 8388864 | tf_op jit(solution)/shard_map/gather | solution.py:39
  94.4 2.7 %gather_fusion.1 = bf16[64,128,256]{2,1,0:T(8,128)(2,1)} fusion(bf16[32,128,256]{2,1,0:T(8,128)(2,1)S(1)} %broadcast_select_fusion, s32[1024]{0:T(1024)S(1)} %get-tuple-element.16), kind=kCustom, calls=%fused_computation.1 | custom fusion | bytes 8388864 | tf_op jit(solution)/shard_map/gather | solution.py:39
  97.1 0.0 copy-start.2
  97.1 7.4 %fusion.5 = f32[64,256,128]{1,2,0:T(8,128)} fusion(bf16[64,128,256]{2,1,0:T(8,128)(2,1)} %gather_fusion.2, bf16[64,4,128,128]{3,2,1,0:T(8,128)(2,1)} %param.13), kind=kOutput, calls=%fused_computation.14 | convolution fusion | flops 536870912 | bytes 14680064 | tf_op jit(solution)/shard_map/tpn,tnf->tpf/dot_general | solution.py:40
  104.6 0.0 copy-done.2
  104.6 6.1 %fusion.7 = f32[64,256,128]{1,2,0:T(8,128)} fusion(bf16[64,128,256]{2,1,0:T(8,128)(2,1)S(1)} %copy-done.2, bf16[64,4,128,128]{3,2,1,0:T(8,128)(2,1)} %param.13), kind=kOutput, calls=%fused_computation.16 | convolution fusion | flops 536870912 | bytes 14680064 | tf_op jit(solution)/shard_map/tpn,tnf->tpf/dot_general | solution.py:40
  110.7 2.8 %gather_fusion.3 = bf16[64,128,256]{2,1,0:T(8,128)(2,1)} fusion(bf16[32,128,256]{2,1,0:T(8,128)(2,1)S(1)} %broadcast_select_fusion, s32[1024]{0:T(1024)S(1)} %get-tuple-element.14), kind=kCustom, calls=%fused_computation.3 | custom fusion | bytes 8388864 | tf_op jit(solution)/shard_map/gather | solution.py:39
  113.4 7.3 %fusion.3 = f32[64,256,128]{1,2,0:T(8,128)} fusion(bf16[64,128,256]{2,1,0:T(8,128)(2,1)} %gather_fusion.3, bf16[64,4,128,128]{3,2,1,0:T(8,128)(2,1)} %param.13), kind=kOutput, calls=%fused_computation.12 | convolution fusion | flops 536870912 | bytes 14680064 | tf_op jit(solution)/shard_map/tpn,tnf->tpf/dot_general | solution.py:40
  120.7 2.8 %gather_fusion.4 = bf16[64,128,256]{2,1,0:T(8,128)(2,1)} fusion(bf16[32,128,256]{2,1,0:T(8,128)(2,1)S(1)} %broadcast_select_fusion, s32[1024]{0:T(1024)S(1)} %get-tuple-element.13), kind=kCustom, calls=%fused_computation.4 | custom fusion | bytes 8388864 | tf_op jit(solution)/shard_map/gather | solution.py:39
  123.5 12.4 %add_convert_fusion = bf16[64,256,128]{1,2,0:T(8,128)(2,1)S(1)} fusion(f32[64,256,128]{1,2,0:T(8,128)} %fusion.3, f32[64,256,128]{1,2,0:T(8,128)} %fusion.5, f32[64,256,128]{1,2,0:T(8,128)} %fusion.7, pred[64]{0:T(512)(128)(4,1)S(1)} %get-tuple-element.11, pred[64]{0:T(512)(128)(4,1)S(1)} %get-tuple-element.12, pred[64]{0:T(512)(128)(4,1)S(1)} %get-tuple-element.10, ...), kind=kOutput, calls=%fused_computation.7 | convolution fusion | flops 553648128 | bytes 35651840 | tf_op jit(solution)/shard_map/tpn,tnf->tpf/dot_general | solution.py:40
  135.9 0.0 copy-done
  135.9 8.1 %fusion.13 = f32[8192,512]{1,0:T(8,128)} fusion(bf16[8192,256]{1,0:T(8,128)(2,1)S(1)} %bitcast.52, bf16[512,512]{1,0:T(8,128)(2,1)S(1)} %copy-done, s32[]{:T(128)S(6)} %select_n.63), kind=kOutput, calls=%fused_computation.23 | convolution fusion | flops 2147483648 | bytes 21233668 | tf_op jit(solution)/shard_map/dot_general | solution.py:50
  144.0 0.0 copy-start.3
  144.0 0.0 copy-start.6
  144.0 0.0 copy-start.7
  144.0 0.0 copy-start.4
  144.0 0.0 copy-start.5
  144.0 0.0 reduce-scatter.2.cloned.1.call-update
  144.0 0.6 copy-done.3
  144.7 0.0 copy-done.6
  144.7 0.0 copy-done.7
  144.7 24.0 %reduce-scatter.2.cloned.1.call-done = f32[4096,512]{1,0:T(8,128)} async-done(((f32[8192,512]{1,0:T(8,128)}), f32[4096,512]{1,0:T(8,128)}) %reduce-scatter.2.cloned.1.call-update) | async-done | bytes 8388624 | tf_op jit(solution)/shard_map/reduce_scatter | solution.py:49
  168.7 0.0 copy-done.4
  168.7 0.0 copy-done.5
  168.7 0.0 copy-start.1
  168.7 6.0 %fusion.1 = bf16[80,4096]{1,0:T(8,128)(2,1)S(1)} fusion(bf16[512,80]{0,1:T(8,128)(2,1)S(1)} %copy-done.5, f32[4096,512]{1,0:T(8,128)} %reduce-scatter.2.cloned.1.call-done, f32[512]{0:T(512)S(1)} %convert_element_type.25, bf16[80,4096]{1,0:T(8,128)(2,1)S(1)} %copy-done.4, f32[80]{0:T(128)S(1)} %convert_element_type.27), kind=kOutput, calls=%fused_computation.10 | convolution fusion | flops 349437952 | bytes 9783616 | tf_op jit(solution)/shard_map/dot_general | solution.py:56
  174.7 0.9 gather_fusion.5
  175.7 4.3 %all_to_all.16 = bf16[2,40,4096]{2,1,0:T(8,128)(2,1)S(1)} all-to-all(bf16[2,40,4096]{2,1,0:T(8,128)(2,1)S(1)} %bitcast.53), channel_id=1, replica_groups=mesh['member'=2,'mesh'=8,'writer'=2] {'writer'}, dimensions={0} | all-to-all | bytes 1310720 | tf_op jit(solution)/shard_map/all_to_all | solution.py:62
  179.9 0.9 copy.26
  180.8 0.0 copy-done.1
  (7 shorter events, 0.0 us)
Async XLA Ops:
  6.5 129.3 %copy-start = (bf16[512,512]{1,0:T(8,128)(2,1)S(1)}, bf16[512,512]{1,0:T(8,128)(2,1)}, u32[]{:S(2)}) copy-start(bf16[512,512]{1,0:T(8,128)(2,1)} %param.17) | copy-start | bytes 1572868
  6.5 79.1 %all-gather.2.cloned.1.call-start = ((), (), s32[]{:S(2)}) async-start(), calls=%async_computation.2 | async-start | bytes 4718592 | tf_op jit(solution)/shard_map/all_gather | solution.py:29
  7.3 161.4 %reduce-scatter.2.cloned.1.call-start = ((), (), s32[]{:S(2)}) async-start(), calls=%async_computation.3 | async-start | bytes 25165824 | tf_op jit(solution)/shard_map/reduce_scatter | solution.py:49
  97.1 7.4 %copy-start.2 = (bf16[64,128,256]{2,1,0:T(8,128)(2,1)S(1)}, bf16[64,128,256]{2,1,0:T(8,128)(2,1)}, u32[]{:S(2)}) copy-start(bf16[64,128,256]{2,1,0:T(8,128)(2,1)} %gather_fusion.1) | copy-start | bytes 12582916
  144.0 0.7 copy-start.3
  144.0 0.7 copy-start.6
  144.0 0.7 copy-start.7
  144.0 24.7 %copy-start.4 = (bf16[80,4096]{1,0:T(8,128)(2,1)S(1)}, bf16[80,4096]{1,0:T(8,128)(2,1)}, u32[]{:S(2)}) copy-start(bf16[80,4096]{1,0:T(8,128)(2,1)} %param.12) | copy-start | bytes 1966084
  144.0 24.7 %copy-start.5 = (bf16[512,80]{0,1:T(8,128)(2,1)S(1)}, bf16[512,80]{0,1:T(8,128)(2,1)}, u32[]{:S(2)}) copy-start(bf16[512,80]{0,1:T(8,128)(2,1)} %param.19) | copy-start | bytes 245764
  168.7 12.1 %copy-start.1 = (bf16[512,512]{1,0:T(8,128)(2,1)S(1)}, bf16[512,512]{1,0:T(8,128)(2,1)}, u32[]{:S(2)}) copy-start(bf16[512,512]{1,0:T(8,128)(2,1)} %param.17) | copy-start | bytes 1572868
Sparse Core Ops, SparseCore 0:
  9.5 76.0 all-gather.1
  144.1 24.5 reduce-scatter.1
where the time goes:
time: 188 us
  waiting for transfers between devices  100 us (53%)
  matrix products  47.3 us (25%)
  local copies, waits for them, and re-layouts  17.8 us (9%)
  between operations  13.5 us (7%)
  other arithmetic  4.65 us (2%)
  blocking collectives  4.26 us (2%)
    all_gather x1, waiting for transfers between devices, local(): block_piece = lax.all_gather(own_blocks, 'mesh', axis=0, tiled=True)  75.5 us
    dot_general x4, matrix products, local(): jnp.einsum('tpn,tnf->tpf', interp[:, slot_col], chosen, preferred_element...  33.2 us
    reduce_scatter x1, waiting for transfers between devices, local(): lax.psum_scatter(jnp.dot(aggregated, weight_rows, preferred_element_type=...  24 us
    gather x4, local copies, waits for them, and re-layouts, local(): chosen = fetched[tile_slots[:, slot_col]]  11.1 us
    dot_general x1, matrix products, local(): jnp.dot(aggregated, weight_rows, preferred_element_type=jnp.float32)  8.09 us
    dot_general x1, matrix products, local(): lax.dot_general(w_out, hidden, (((0,), (1,)), ((), ())), preferred_elemen...  6.01 us
    all_to_all x1, blocking collectives, local(): lax.all_to_all(ordered, 'writer', split_axis=0, concat_axis=1, tiled=True)  4.26 us
    gather x1, local copies, waits for them, and re-layouts, local(): picked = block_piece[offset_ids]  4.21 us
  transfers between devices with their start and end apart: 2, of which 2 were waited for; matrix products, arithmetic and copies ran while one was open for 2% of the time, Pallas kernels for 0%

commit v1 on v0

v1 whole, which is shorter than its diff:
```python
import jax
import jax.numpy as jnp
from jax import lax
from jax.experimental import pallas as pl
from jax.experimental.pallas import tpu as pltpu
from jax.sharding import PartitionSpec as P

BLK = 128
K = 4
META = 8


def ring_position(index, count, columns):
    if columns == 1:
        return index
    row, column = index // 2, index % 2
    return jnp.where(column == 0, row, count - 1 - row)


def ring_order(count, columns):
    if columns == 1:
        return list(range(count))
    return list(range(0, count, 2)) + list(range(count - 1, 0, -2))


def decode_kernel(stage, blocks, pieces, tiles, *refs):
    meta, w_in, b_in, w_out, b_out, interp = refs[:6]
    piece_refs = refs[6 : 6 + 2 * len(pieces)]
    own_out, other_out, x_buf, a_buf, g_buf, o_buf, order, in_sem, out_sem = refs[
        8 + 2 * len(pieces) :
    ]
    half = piece_refs[0].shape[1]
    rows = own_out.shape[0]

    def columns_of(tile):
        return pl.ds(pl.multiple_of(tile * BLK, BLK), BLK)

    def grid_copies(tile, i):
        return [
            pltpu.make_async_copy(ref.at[:, columns_of(tile)], g_buf.at[i, pl.ds(j * rows, rows)], in_sem.at[i])
            for j, ref in enumerate((own_out, other_out))
        ]

    def out_copies(tile, i):
        return [
            pltpu.make_async_copy(o_buf.at[i, pl.ds(j * rows, rows)], ref.at[:, columns_of(tile)], out_sem)
            for j, ref in enumerate((own_out, other_out))
        ]

    def weight_copy(tile, i, k):
        return pltpu.make_async_copy(
            interp.at[meta[tile * META + K + 2], k], a_buf.at[i, :, pl.ds(k * BLK, BLK)], in_sem.at[i]
        )

    def node_copies(j, row, i, k):
        source = pl.ds(pl.multiple_of(row, BLK), BLK)
        return [
            pltpu.make_async_copy(
                piece_refs[2 * j + h].at[source],
                x_buf.at[i, pl.ds(k * BLK, BLK), pl.ds(h * half, half)],
                in_sem.at[i],
            )
            for h in range(2)
        ]

    def fetch(tile, i):
        live = meta[tile * META + K]
        for copy in grid_copies(tile, i):
            copy.start()
        for k in range(K):

            @pl.when(k < live)
            def _():
                weight_copy(tile, i, k).start()
                code = meta[tile * META + k]
                piece, row = code // blocks, (code % blocks) * BLK
                for j, where in enumerate(pieces):

                    @pl.when(piece == where)
                    def _():
                        for copy in node_copies(j, row, i, k):
                            copy.start()

            @pl.when(k >= live)
            def _():
                a_buf[i, :, k * BLK : (k + 1) * BLK] = jnp.zeros((BLK, BLK), jnp.bfloat16)
                x_buf[i, k * BLK : (k + 1) * BLK, :] = jnp.zeros((BLK, 2 * half), jnp.bfloat16)

    def arrive(i):
        tile = order[i]
        live = meta[tile * META + K]
        for copy in grid_copies(tile, i):
            copy.wait()
        for k in range(K):

            @pl.when(k < live)
            def _():
                weight_copy(tile, i, k).wait()
                for copy in node_copies(0, 0, i, k):
                    copy.wait()

    def scan(tile, count):
        mine = meta[tile * META + K + 1] == stage

        @pl.when(mine)
        def _():
            order[count] = tile
            fetch(tile, count)

        return count + mine.astype(jnp.int32)

    count = lax.fori_loop(0, tiles, scan, jnp.int32(0))

    def pair(g, _):
        for j in range(2):

            @pl.when(2 * g + j < count)
            def _():
                arrive(2 * g + j)

        aggregated = jnp.concatenate(
            [
                jnp.dot(a_buf[2 * g + j], x_buf[2 * g + j], preferred_element_type=jnp.float32).astype(jnp.bfloat16)
                for j in range(2)
            ],
            axis=0,
        )
        layer = jnp.dot(aggregated, w_in[...], preferred_element_type=jnp.float32) + b_in[...]
        hidden = (layer * (0.5 * jnp.tanh(0.5 * layer) + 0.5)).astype(jnp.bfloat16)
        decoded = lax.dot_general(
            w_out[...], hidden, (((1,), (1,)), ((), ())), preferred_element_type=jnp.float32
        )
        decoded = decoded + b_out[...]
        for j in range(2):
            i = 2 * g + j
            o_buf[i] = (g_buf[i].astype(jnp.float32) + decoded[:, j * BLK : (j + 1) * BLK]).astype(jnp.bfloat16)
        for j in range(2):

            @pl.when(2 * g + j < count)
            def _():
                for copy in out_copies(order[2 * g + j], 2 * g + j):
                    copy.start()

        return 0

    lax.fori_loop(0, (count + 1) // 2, pair, 0)

    def drain(i, _):
        for copy in out_copies(order[i], i):
            copy.wait()
        return 0

    lax.fori_loop(0, count, drain, 0)


def decode_tiles(stage, blocks, pieces, tiles, small, interp, arrays, outs):
    meta, w_in, b_in, w_out, b_out = small
    flat = [half for pair in arrays for half in pair]
    half = flat[0].shape[1]
    rows = outs[0].shape[0]
    vmem, anywhere = pl.BlockSpec(memory_space=pltpu.VMEM), pl.BlockSpec(memory_space=pl.ANY)
    first_out = 6 + len(flat)
    slots = tiles + tiles % 2
    share = max(tiles // 4, 1)
    return pl.pallas_call(
        lambda *refs: decode_kernel(stage, blocks, pieces, tiles, *refs),
        out_shape=[jax.ShapeDtypeStruct(out.shape, out.dtype) for out in outs],
        in_specs=[pl.BlockSpec(memory_space=pltpu.SMEM)] + [vmem] * 4 + [anywhere] * (1 + len(flat) + 2),
        out_specs=[anywhere] * 2,
        input_output_aliases={first_out: 0, first_out + 1: 1},
        scratch_shapes=[
            pltpu.VMEM((slots, K * BLK, 2 * half), jnp.bfloat16),
            pltpu.VMEM((slots, BLK, K * BLK), jnp.bfloat16),
            pltpu.VMEM((slots, 2 * rows, BLK), jnp.bfloat16),
            pltpu.VMEM((slots, 2 * rows, BLK), jnp.bfloat16),
            pltpu.SMEM((slots,), jnp.int32),
            pltpu.SemaphoreType.DMA((slots,)),
            pltpu.SemaphoreType.DMA,
        ],
        compiler_params=pltpu.CompilerParams(vmem_limit_bytes=48 * 2**20),
        cost_estimate=pl.CostEstimate(
            flops=share * BLK * 2 * (K * BLK * 2 * half + 4 * half * half + 4 * half * rows),
            bytes_accessed=share * 6 * BLK * BLK * 10,
            transcendentals=share * BLK * 2 * half,
        ),
        name="decode_tiles",
    )(meta, w_in, b_in, w_out, b_out, interp, *flat, *outs)


def make_local(count):
    columns = 2 if count == 8 else 1
    far = count // 2
    ring = ring_order(count, columns)
    onward = []
    for place in range(count):
        onward.append((ring[place] * 2, ring[(place + 1) % count] * 2))
        onward.append((ring[place] * 2 + 1, ring[(place - 1) % count] * 2 + 1))

    def send_on(piece):
        return lax.ppermute(piece, ("mesh", "writer"), onward)

    def swap(piece):
        return lax.ppermute(piece, "writer", [(0, 1), (1, 0)])

    def local(
        mesh_nodes,
        grid_state,
        interp,
        wanted,
        tile_slots,
        edge_count,
        w_in,
        b_in,
        w_out,
        b_out,
        writer_order,
    ):
        nodes, half = mesh_nodes.shape
        blocks = nodes // BLK
        core = lax.axis_index("writer")
        tiles = interp.shape[0] // 2
        channels = w_out.shape[1]
        each = channels // 2
        rows = -(-each // 16) * 16

        first_tile = core * tiles
        slots = lax.dynamic_slice_in_dim(tile_slots, first_tile, tiles, 0)
        live = lax.dynamic_slice_in_dim(edge_count, first_tile, tiles, 0)
        ids = wanted[0]
        here = ring_position(lax.axis_index("mesh"), count, columns)
        behind = here - ring_position(ids // blocks, count, columns)
        behind = jnp.mod(jnp.where(core == 0, behind, -behind), count)
        codes_listed = behind * blocks + ids % blocks
        chosen = slots[:, :, None] == jnp.arange(ids.shape[0])
        codes = jnp.sum(jnp.where(chosen, codes_listed, 0), axis=2)
        piece = codes // blocks
        distance = jnp.minimum(piece, count - piece)
        distance = jnp.max(jnp.where(jnp.arange(K) < live[:, None], distance, 0), axis=1)
        stages = [d for d in range(max(far - 3, 1), far + 1)]
        stage_of = jnp.maximum(distance, stages[0])
        numbers = first_tile + jnp.arange(tiles, dtype=jnp.int32)
        meta = jnp.concatenate(
            [codes, live[:, None], stage_of[:, None], numbers[:, None], jnp.zeros((tiles, 1), jnp.int32)], axis=1
        ).astype(jnp.int32).reshape(-1)

        weights = jnp.where(core == 0, w_in, jnp.roll(w_in, -half, axis=0))
        picks = jnp.where(core == 0, writer_order, jnp.roll(writer_order, -each))
        pad = jnp.broadcast_to(picks[:1], (rows - each,))
        picks = jnp.concatenate([picks[:each], pad, picks[each:], pad])
        heads = w_out.T[picks]
        head_bias = b_out.astype(jnp.float32)[picks][:, None]
        small = (meta, weights, b_in.astype(jnp.float32)[None], heads, head_bias)
        state = grid_state[picks]
        outs = [state[:rows], state[rows:]]

        other_nodes = swap(mesh_nodes)
        same, cross = [mesh_nodes], [other_nodes]
        table = {0: (mesh_nodes, other_nodes)}
        for d in range(1, far + 1):
            cross.append(send_on(cross[-1]))
            if d < far:
                same.append(send_on(same[-1]))
                table[d] = (same[d], cross[d])
                table[count - d] = (swap(cross[d]), swap(same[d]))
            else:
                table[d] = (swap(cross[d]), cross[d])
            if d in stages:
                pieces = sorted(table)
                outs = decode_tiles(
                    d, blocks, pieces, tiles, small, interp, [table[p] for p in pieces], outs
                )
        received = swap(outs[1])
        own, received = outs[0][:each], received[:each]
        return jnp.concatenate(
            [jnp.where(core == 0, own, received), jnp.where(core == 0, received, own)], axis=1
        )

    return local


def solution(mesh):
    placed = (
        P(("member", "mesh"), "writer"),
        P(None, ("member", "mesh", "writer")),
        P("mesh", None, None, None),
        P("mesh", None),
        P("mesh", None),
        P("mesh"),
        P(),
        P(),
        P(),
        P(),
        P(),
    )
    return jax.shard_map(
        make_local(mesh.shape["mesh"]),
        mesh=mesh,
        in_specs=placed,
        out_specs=P("writer", ("member", "mesh")),
        check_vma=False,
    )
```

time: 188 us -> 82.6 us (0.44)
  waiting for transfers between devices: 100 us -> 19.1 us
  matrix products: 47.3 us -> 0 us
  Pallas kernels: 0 us -> 23.7 us
  starting transfers between devices: 0.04 us -> 17.8 us
  between operations: 13.5 us -> 0.23 us
  blocking collectives: 4.26 us -> 0 us
    all_gather x1 -> x0, waiting for transfers between devices: 75.5 us -> none  [local(): block_piece = lax.all_gather(own_blocks, 'mesh', axis=0, tiled=True)]
    dot_general x6 -> x0, matrix products: 47.3 us -> none  [the longest x4 33.2 us: local(): jnp.einsum('tpn,tnf->tpf', interp[:, slot_col], chosen, preferred_element...]
    reduce_scatter x1 -> x0, waiting for transfers between devices: 24 us -> none  [local(): lax.psum_scatter(jnp.dot(aggregated, weight_rows, preferred_element_type=...]
    pallas_call x0 -> x4, Pallas kernels: none -> 23.7 us  [decode_tiles(): pl.pallas_call(lambda *refs: decode_kernel(stage, blocks, pieces, tiles,...]
    ppermute x0 -> x16, waiting for transfers between devices: none -> 19.1 us  [the longest x7 17.7 us: send_on(): return lax.ppermute(piece, ('mesh', 'writer'), onward)]
    ppermute x0 -> x16, starting transfers between devices: none -> 17.8 us  [the longest x7 14.1 us: send_on(): return lax.ppermute(piece, ('mesh', 'writer'), onward)]
    gather x6 -> x3, local copies, waits for them, and re-layouts: 16.2 us -> 6.01 us  [the longest x1 2.32 us: local(): heads = w_out.T[picks]]
    all_to_all x1 -> x0, blocking collectives: 4.26 us -> none  [local(): lax.all_to_all(ordered, 'writer', split_axis=0, concat_axis=1, tiled=True)]
  transfers between devices with their start and end apart: 2 -> 16, of which waited for: 2 -> 6; matrix products, arithmetic and copies ran while one was open for 2% -> 22% of each run, Pallas kernels for 0% -> 24%
where the time goes in v1:
time: 82.6 us; the launch traced here: 81.4 us
  Pallas kernels  23.7 us (29%)
  waiting for transfers between devices  19.1 us (23%)
  starting transfers between devices  17.8 us (22%)
  local copies, waits for them, and re-layouts  16.1 us (19%)
  other arithmetic  4.51 us (5%)
    pallas_call x4, Pallas kernels, decode_tiles(): pl.pallas_call(lambda *refs: decode_kernel(stage, blocks, pieces, tiles,...  23.7 us
    ppermute x7, waiting for transfers between devices, send_on(): return lax.ppermute(piece, ('mesh', 'writer'), onward)  17.7 us
    ppermute x7, starting transfers between devices, send_on(): return lax.ppermute(piece, ('mesh', 'writer'), onward)  14.1 us
    ppermute x9, starting transfers between devices, swap(): return lax.ppermute(piece, 'writer', [(0, 1), (1, 0)])  3.68 us
    gather x1, local copies, waits for them, and re-layouts, local(): heads = w_out.T[picks]  2.32 us
    gather x1, local copies, waits for them, and re-layouts, local(): state = grid_state[picks]  1.94 us
    gather x1, local copies, waits for them, and re-layouts, local(): head_bias = b_out.astype(jnp.float32)[picks][:, None]  1.75 us
  transfers between devices with their start and end apart: 16, of which 6 were waited for; matrix products, arithmetic and copies ran while one was open for 22% of the time, Pallas kernels for 24%

profile of v1, /device:TPU:0, one launch (start us, length us, event | category | flops | bytes accessed | tf_op | source)
XLA Modules:
  0.0 81.4 jit_solution(5637858613209017999)
XLA Ops:
  0.0 0.5 collective-permute-start
  0.5 2.6 %collective-permute-start.1 = (bf16[1024,256]{1,0:T(8,128)(2,1)}, bf16[1024,256]{1,0:T(8,128)(2,1)S(1)}, u32[]{:S(2)}, u32[]{:S(2)}) collective-permute-start(bf16[1024,256]{1,0:T(8,128)(2,1)} %refs_6_.7), channel_id=1, source_target_pairs={{0,4},{1,3},{4,8},{5,1},{8,12},{9,5},{12,14},{13,9},{14,10},{15,13... | collective-permute-start | bytes 1572872 | tf_op jit(solution)/shard_map/ppermute | solution.py:200
  3.1 0.8 fusion.10
  3.9 1.6 %collective-permute-start.2 = (bf16[1024,256]{1,0:T(8,128)(2,1)S(1)}, bf16[1024,256]{1,0:T(8,128)(2,1)S(1)}, u32[]{:S(2)}, u32[]{:S(2)}) collective-permute-start(bf16[1024,256]{1,0:T(8,128)(2,1)S(1)} %collective-permute-done.refs_7_), channel_id=1, source_target_pairs={{0,4},{1,3},{4,8},{5,1},{8,12},{9,5},{12,14},{13,9},{14,10},{15,13... | collective-permute-start | bytes 1572872 | tf_op jit(solution)/shard_map/ppermute | solution.py:200
  5.5 0.7 broadcast_select_fusion.2
  6.2 0.7 dynamic_slice.7
  6.9 0.1 slice_bitcast_fusion.1
  7.0 0.1 fusion.7
  7.1 1.9 %gather_fusion.2 = bf16[96,4096]{1,0:T(8,128)(2,1)} fusion(bf16[80,4096]{1,0:T(8,128)(2,1)S(1)} %copy-done, s32[1024]{0:T(1024)S(1)} %pad_clamp_fusion), kind=kCustom, calls=%fused_computation.2 | custom fusion | bytes 1573248 | tf_op jit(solution)/shard_map/gather | solution.py:253
  9.1 6.9 %collective-permute-done.2.refs_9_ = bf16[1024,256]{1,0:T(8,128)(2,1)S(1)} collective-permute-done((bf16[1024,256]{1,0:T(8,128)(2,1)S(1)}, bf16[1024,256]{1,0:T(8,128)(2,1)S(1)}, u32[]{:S(2)}, u32[]{:S(2)}) %collective-permute-start.2) | collective-permute-done | bytes 524320 | tf_op jit(solution)/shard_map/ppermute | solution.py:200
  16.0 2.1 %collective-permute-start.4 = (bf16[1024,256]{1,0:T(8,128)(2,1)S(1)}, bf16[1024,256]{1,0:T(8,128)(2,1)}, u32[]{:S(2)}, u32[]{:S(2)}) collective-permute-start(bf16[1024,256]{1,0:T(8,128)(2,1)S(1)} %collective-permute-done.2.refs_9_), channel_id=1, source_target_pairs={{0,4},{1,3},{4,8},{5,1},{8,12},{9,5},{12,14},{13,9},{14,10},{15,13... | collective-permute-start | bytes 1572872 | tf_op jit(solution)/shard_map/ppermute | solution.py:200
  18.1 1.2 %fusion.8 = (bf16[48,4096]{1,0:T(8,128)(2,1)S(1)}, bf16[48,4096]{1,0:T(8,128)(2,1)S(1)}) fusion(bf16[96,4096]{1,0:T(8,128)(2,1)} %gather_fusion.2), kind=kLoop, calls=%fused_computation.48 | loop fusion | bytes 1572864 | tf_op jit(solution)/shard_map/slice | solution.py:254
  19.3 1.6 %collective-permute-start.3 = (bf16[1024,256]{1,0:T(8,128)(2,1)S(1)}, bf16[1024,256]{1,0:T(8,128)(2,1)}, u32[]{:S(2)}, u32[]{:S(2)}) collective-permute-start(bf16[1024,256]{1,0:T(8,128)(2,1)S(1)} %collective-permute-done.1.refs_8_), channel_id=1, source_target_pairs={{0,4},{1,3},{4,8},{5,1},{8,12},{9,5},{12,14},{13,9},{14,10},{15,13... | collective-permute-start | bytes 1572872 | tf_op jit(solution)/shard_map/ppermute | solution.py:200
  20.9 4.4 %collective-permute-done.4.refs_11_ = bf16[1024,256]{1,0:T(8,128)(2,1)} collective-permute-done((bf16[1024,256]{1,0:T(8,128)(2,1)S(1)}, bf16[1024,256]{1,0:T(8,128)(2,1)}, u32[]{:S(2)}, u32[]{:S(2)}) %collective-permute-start.4) | collective-permute-done | bytes 524320 | tf_op jit(solution)/shard_map/ppermute | solution.py:200
  25.3 2.1 %collective-permute-start.6 = (bf16[1024,256]{1,0:T(8,128)(2,1)}, bf16[1024,256]{1,0:T(8,128)(2,1)}, u32[]{:S(2)}, u32[]{:S(2)}) collective-permute-start(bf16[1024,256]{1,0:T(8,128)(2,1)} %collective-permute-done.4.refs_11_), channel_id=1, source_target_pairs={{0,4},{1,3},{4,8},{5,1},{8,12},{9,5},{12,14},{13,9},{14,10},{15,13... | collective-permute-start | bytes 1572872 | tf_op jit(solution)/shard_map/ppermute | solution.py:200
  27.4 0.1 constant_dynamic-slice_fusion
  27.5 0.2 select_reduce_fusion
  27.7 0.1 collective-permute-start.14
  27.8 0.6 collective-permute-start.13
  28.4 2.6 %collective-permute-done.3.refs_10_ = bf16[1024,256]{1,0:T(8,128)(2,1)} collective-permute-done((bf16[1024,256]{1,0:T(8,128)(2,1)S(1)}, bf16[1024,256]{1,0:T(8,128)(2,1)}, u32[]{:S(2)}, u32[]{:S(2)}) %collective-permute-start.3) | collective-permute-done | bytes 524320 | tf_op jit(solution)/shard_map/ppermute | solution.py:200
  30.9 2.1 %collective-permute-start.5 = (bf16[1024,256]{1,0:T(8,128)(2,1)}, bf16[1024,256]{1,0:T(8,128)(2,1)}, u32[]{:S(2)}, u32[]{:S(2)}) collective-permute-start(bf16[1024,256]{1,0:T(8,128)(2,1)} %collective-permute-done.3.refs_10_), channel_id=1, source_target_pairs={{0,4},{1,3},{4,8},{5,1},{8,12},{9,5},{12,14},{13,9},{14,10},{15,13... | collective-permute-start | bytes 1572872 | tf_op jit(solution)/shard_map/ppermute | solution.py:200
  33.0 3.5 %collective-permute-done.6.refs_13_ = bf16[1024,256]{1,0:T(8,128)(2,1)} collective-permute-done((bf16[1024,256]{1,0:T(8,128)(2,1)}, bf16[1024,256]{1,0:T(8,128)(2,1)}, u32[]{:S(2)}, u32[]{:S(2)}) %collective-permute-start.6) | collective-permute-done | bytes 524320 | tf_op jit(solution)/shard_map/ppermute | solution.py:200
  36.5 2.1 %collective-permute-start.7 = (bf16[1024,256]{1,0:T(8,128)(2,1)}, bf16[1024,256]{1,0:T(8,128)(2,1)}, u32[]{:S(2)}, u32[]{:S(2)}) collective-permute-start(bf16[1024,256]{1,0:T(8,128)(2,1)} %collective-permute-done.6.refs_13_), channel_id=1, source_target_pairs={{0,4},{1,3},{4,8},{5,1},{8,12},{9,5},{12,14},{13,9},{14,10},{15,13... | collective-permute-start | bytes 1572872 | tf_op jit(solution)/shard_map/ppermute | solution.py:200
  38.6 0.6 maximum_bitcast_fusion
  39.2 0.8 %fusion.9 = (bf16[256,512]{1,0:T(8,128)(2,1)}, bf16[256,512]{1,0:T(8,128)(2,1)}) fusion(bf16[512,512]{1,0:T(8,128)(2,1)S(1)} %copy-done.8), kind=kLoop, calls=%fused_computation.49 | loop fusion | bytes 1048576 | tf_op jit(solution)/shard_map/jit(_roll_static)/slice | solution.py:246
  40.1 0.8 copy-done.2
  40.8 0.5 collective-permute-start.11
  41.4 0.5 iota_add_fusion
  41.9 0.3 collective-permute-done.5.refs_12_
  42.2 0.8 copy-done.4
  43.0 0.5 collective-permute-start.9
  43.5 0.7 dynamic-slice_bitcast_fusion
  44.1 1.8 %gather_fusion.1 = f32[96]{0:T(128)} fusion(f32[80]{0:T(128)S(1)} %convert_element_type.4, s32[1024]{0:T(1024)S(1)} %pad_clamp_fusion), kind=kCustom, calls=%fused_computation.1 | custom fusion | bytes 1152 | tf_op jit(solution)/shard_map/gather | solution.py:251
  45.9 0.6 broadcast_in_dim.43
  46.5 0.7 concatenate.40
  47.2 0.7 copy.40
  47.8 0.8 reshape.142.refs_0_
  48.7 1.3 %copy.44.refs_4_ = f32[96,1]{1,0:T(8,128)} copy(f32[96,1]{0,1:T(1,128)} %bitcast.34) | data formatting | bytes 768 | tf_op jit(solution)/shard_map/broadcast_in_dim | solution.py:251
  50.0 2.3 %gather_fusion = bf16[96,512]{1,0:T(8,128)(2,1)} fusion(bf16[80,512]{1,0:T(8,128)(2,1)} %bitcast.32, s32[1024]{0:T(1024)S(1)} %pad_clamp_fusion), kind=kCustom, calls=%fused_computation | custom fusion | bytes 196992 | tf_op jit(solution)/shard_map/gather | solution.py:250
  52.3 0.1 collective-permute-start.8
  52.4 1.4 %maximum_select_fusion.refs_1_ = bf16[512,512]{1,0:T(8,128)(2,1)S(1)} fusion(bf16[512,512]{1,0:T(8,128)(2,1)} %param.17, bf16[256,512]{1,0:T(8,128)(2,1)} %get-tuple-element.26, bf16[256,512]{1,0:T(8,128)(2,1)} %get-tuple-element.25, pred[]{:T(512)S(6)} %eq.18), kind=kLoop, calls=%fused_computation.4 | loop fusion | flops 1310720 | bytes 1572865 | tf_op jit(solution)/shard_map/jit(_where)/select_n | solution.py:246
  53.9 4.5 %decode_tiles.4 = (bf16[48,4096]{1,0:T(8,128)(2,1)S(1)}, bf16[48,4096]{1,0:T(8,128)(2,1)S(1)}) custom-call(s32[256]{0:T(256)S(1)} %reshape.142.refs_0_, bf16[512,512]{1,0:T(8,128)(2,1)S(1)} %maximum_select_fusion.refs_1_, f32[1,512]{1,0:T(1,128)S(1)} %bitcast.28, bf16[96,512]{1,0:T(8,128)(2,1)S(1)} %copy-done.6, ...), custom_call_target="tpu_custom_call", output_to_operand_aliasing={{0}: (12, {}), {1}: (13, {})} | custom-call | flops 1174405120 | bytes 7864320 | tf_op jit(solution)/shard_map/decode_tiles/pallas_call | solution.py:165
  58.4 6.8 %decode_tiles.5 = (bf16[48,4096]{1,0:T(8,128)(2,1)S(1)}, bf16[48,4096]{1,0:T(8,128)(2,1)S(1)}) custom-call(s32[256]{0:T(256)S(1)} %reshape.142.refs_0_, bf16[512,512]{1,0:T(8,128)(2,1)S(1)} %maximum_select_fusion.refs_1_, f32[1,512]{1,0:T(1,128)S(1)} %bitcast.29, bf16[96,512]{1,0:T(8,128)(2,1)S(1)} %copy-done.6, ...), custom_call_target="tpu_custom_call", output_to_operand_aliasing={{0}: (16, {}), {1}: (17, {})} | custom-call | flops 1174405120 | bytes 7864320 | tf_op jit(solution)/shard_map/decode_tiles/pallas_call | solution.py:165
  65.2 8.5 %decode_tiles.6 = (bf16[48,4096]{1,0:T(8,128)(2,1)S(1)}, bf16[48,4096]{1,0:T(8,128)(2,1)S(1)}) custom-call(s32[256]{0:T(256)S(1)} %reshape.142.refs_0_, bf16[512,512]{1,0:T(8,128)(2,1)S(1)} %maximum_select_fusion.refs_1_, f32[1,512]{1,0:T(1,128)S(1)} %bitcast.30, bf16[96,512]{1,0:T(8,128)(2,1)S(1)} %copy-done.6, ...), custom_call_target="tpu_custom_call", output_to_operand_aliasing={{0}: (20, {}), {1}: (21, {})} | custom-call | flops 1174405120 | bytes 7864320 | tf_op jit(solution)/shard_map/decode_tiles/pallas_call | solution.py:165
  73.8 3.9 %decode_tiles.7 = (bf16[48,4096]{1,0:T(8,128)(2,1)S(1)}, bf16[48,4096]{1,0:T(8,128)(2,1)S(1)}) custom-call(s32[256]{0:T(256)S(1)} %reshape.142.refs_0_, bf16[512,512]{1,0:T(8,128)(2,1)S(1)} %maximum_select_fusion.refs_1_, f32[1,512]{1,0:T(1,128)S(1)} %bitcast.31, bf16[96,512]{1,0:T(8,128)(2,1)S(1)} %copy-done.6, ...), custom_call_target="tpu_custom_call", output_to_operand_aliasing={{0}: (22, {}), {1}: (23, {})} | custom-call | flops 1174405120 | bytes 7864320 | tf_op jit(solution)/shard_map/decode_tiles/pallas_call | solution.py:165
  77.6 1.5 %collective-permute-start.15 = (bf16[48,4096]{1,0:T(8,128)(2,1)S(1)}, bf16[48,4096]{1,0:T(8,128)(2,1)S(1)}, u32[]{:S(2)}, u32[]{:S(2)}) collective-permute-start(bf16[48,4096]{1,0:T(8,128)(2,1)S(1)} %get-tuple-element.20), channel_id=1, source_target_pairs={{0,1},{1,0},{2,3},{3,2},{4,5},{5,4},{6,7},{7,6},{8,9},{9,8},{10,11... | collective-permute-start | bytes 1179656 | tf_op jit(solution)/shard_map/ppermute | solution.py:203
  79.1 1.3 %collective-permute-done.15 = bf16[48,4096]{1,0:T(8,128)(2,1)S(1)} collective-permute-done((bf16[48,4096]{1,0:T(8,128)(2,1)S(1)}, bf16[48,4096]{1,0:T(8,128)(2,1)S(1)}, u32[]{:S(2)}, u32[]{:S(2)}) %collective-permute-start.15) | collective-permute-done | bytes 393248 | tf_op jit(solution)/shard_map/ppermute | solution.py:203
  80.5 0.9 %pad_maximum_fusion = bf16[40,8192]{1,0:T(8,128)(2,1)} fusion(bf16[40,4096]{1,0:T(8,128)(2,1)S(1)} %get-tuple-element.22, bf16[40,4096]{1,0:T(8,128)(2,1)S(1)} %get-tuple-element.21), kind=kLoop, calls=%fused_computation.3 | loop fusion | flops 1310720 | bytes 1310720 | tf_op jit(solution)/shard_map/concatenate | solution.py:274
  (45 shorter events, 0.2 us)
Async XLA Ops:
  0.0 7.1 %copy-start = (bf16[80,4096]{1,0:T(8,128)(2,1)S(1)}, bf16[80,4096]{1,0:T(8,128)(2,1)}, u32[]{:S(2)}) copy-start(bf16[80,4096]{1,0:T(8,128)(2,1)} %param.12) | copy-start | bytes 1966084
  0.0 3.9 %collective-permute-start = (bf16[1024,256]{1,0:T(8,128)(2,1)}, bf16[1024,256]{1,0:T(8,128)(2,1)S(1)}, u32[]{:S(2)}, u32[]{:S(2)}) collective-permute-start(bf16[1024,256]{1,0:T(8,128)(2,1)} %refs_6_.7), channel_id=1, source_target_pairs={{0,1},{1,0},{2,3},{3,2},{4,5},{5,4},{6,7},{7,6},{8,9},{9,8},{10,11... | collective-permute-start | bytes 1572872 | tf_op jit(solution)/shard_map/ppermute | solution.py:203
  0.5 18.8 %collective-permute-start.1 = (bf16[1024,256]{1,0:T(8,128)(2,1)}, bf16[1024,256]{1,0:T(8,128)(2,1)S(1)}, u32[]{:S(2)}, u32[]{:S(2)}) collective-permute-start(bf16[1024,256]{1,0:T(8,128)(2,1)} %refs_6_.7), channel_id=1, source_target_pairs={{0,4},{1,3},{4,8},{5,1},{8,12},{9,5},{12,14},{13,9},{14,10},{15,13... | collective-permute-start | bytes 1572872 | tf_op jit(solution)/shard_map/ppermute | solution.py:200
  3.9 12.1 %collective-permute-start.2 = (bf16[1024,256]{1,0:T(8,128)(2,1)S(1)}, bf16[1024,256]{1,0:T(8,128)(2,1)S(1)}, u32[]{:S(2)}, u32[]{:S(2)}) collective-permute-start(bf16[1024,256]{1,0:T(8,128)(2,1)S(1)} %collective-permute-done.refs_7_), channel_id=1, source_target_pairs={{0,4},{1,3},{4,8},{5,1},{8,12},{9,5},{12,14},{13,9},{14,10},{15,13... | collective-permute-start | bytes 1572872 | tf_op jit(solution)/shard_map/ppermute | solution.py:200
  9.1 18.3 %copy-start.9 = (s32[64,4]{0,1:T(4,128)S(1)}, s32[64,4]{0,1:T(4,128)}, u32[]{:S(2)}) copy-start(s32[64,4]{0,1:T(4,128)} %param.15) | copy-start | bytes 3076
  9.1 18.4 %copy-start.11 = (s32[1,32]{1,0:T(1,128)S(1)}, s32[1,32]{1,0:T(1,128)}, u32[]{:S(2)}) copy-start(s32[1,32]{1,0:T(1,128)} %param.14) | copy-start | bytes 388
  9.1 30.1 %copy-start.8 = (bf16[512,512]{1,0:T(8,128)(2,1)S(1)}, bf16[512,512]{1,0:T(8,128)(2,1)}, u32[]{:S(2)}) copy-start(bf16[512,512]{1,0:T(8,128)(2,1)} %param.17) | copy-start | bytes 1572868
  9.1 34.4 %copy-start.12 = (s32[64]{0:T(128)S(1)}, s32[64]{0:T(128)}, u32[]{:S(2)}) copy-start(s32[64]{0:T(128)} %param.16) | copy-start | bytes 772
  9.1 35.0 %copy-start.13 = (bf16[80]{0:T(256)(128)(2,1)S(1)}, bf16[80]{0:T(256)(128)(2,1)}, u32[]{:S(2)}) copy-start(bf16[80]{0:T(256)(128)(2,1)} %param.20) | copy-start | bytes 484
  9.1 35.0 %copy-start.10 = (bf16[512]{0:T(512)(128)(2,1)S(1)}, bf16[512]{0:T(512)(128)(2,1)}, u32[]{:S(2)}) copy-start(bf16[512]{0:T(512)(128)(2,1)} %param.18) | copy-start | bytes 3076
  16.0 9.3 %collective-permute-start.4 = (bf16[1024,256]{1,0:T(8,128)(2,1)S(1)}, bf16[1024,256]{1,0:T(8,128)(2,1)}, u32[]{:S(2)}, u32[]{:S(2)}) collective-permute-start(bf16[1024,256]{1,0:T(8,128)(2,1)S(1)} %collective-permute-done.2.refs_9_), channel_id=1, source_target_pairs={{0,4},{1,3},{4,8},{5,1},{8,12},{9,5},{12,14},{13,9},{14,10},{15,13... | collective-permute-start | bytes 1572872 | tf_op jit(solution)/shard_map/ppermute | solution.py:200
  19.3 11.7 %collective-permute-start.3 = (bf16[1024,256]{1,0:T(8,128)(2,1)S(1)}, bf16[1024,256]{1,0:T(8,128)(2,1)}, u32[]{:S(2)}, u32[]{:S(2)}) collective-permute-start(bf16[1024,256]{1,0:T(8,128)(2,1)S(1)} %collective-permute-done.1.refs_8_), channel_id=1, source_target_pairs={{0,4},{1,3},{4,8},{5,1},{8,12},{9,5},{12,14},{13,9},{14,10},{15,13... | collective-permute-start | bytes 1572872 | tf_op jit(solution)/shard_map/ppermute | solution.py:200
  25.3 11.2 %collective-permute-start.6 = (bf16[1024,256]{1,0:T(8,128)(2,1)}, bf16[1024,256]{1,0:T(8,128)(2,1)}, u32[]{:S(2)}, u32[]{:S(2)}) collective-permute-start(bf16[1024,256]{1,0:T(8,128)(2,1)} %collective-permute-done.4.refs_11_), channel_id=1, source_target_pairs={{0,4},{1,3},{4,8},{5,1},{8,12},{9,5},{12,14},{13,9},{14,10},{15,13... | collective-permute-start | bytes 1572872 | tf_op jit(solution)/shard_map/ppermute | solution.py:200
  27.7 12.3 %collective-permute-start.14 = (bf16[1024,256]{1,0:T(8,128)(2,1)S(1)}, bf16[1024,256]{1,0:T(8,128)(2,1)S(1)}, u32[]{:S(2)}, u32[]{:S(2)}) collective-permute-start(bf16[1024,256]{1,0:T(8,128)(2,1)S(1)} %collective-permute-done.1.refs_8_), channel_id=1, source_target_pairs={{0,1},{1,0},{2,3},{3,2},{4,5},{5,4},{6,7},{7,6},{8,9},{9,8},{10,11... | collective-permute-start | bytes 1572872 | tf_op jit(solution)/shard_map/ppermute | solution.py:203
  27.8 14.4 %collective-permute-start.13 = (bf16[1024,256]{1,0:T(8,128)(2,1)S(1)}, bf16[1024,256]{1,0:T(8,128)(2,1)S(1)}, u32[]{:S(2)}, u32[]{:S(2)}) collective-permute-start(bf16[1024,256]{1,0:T(8,128)(2,1)S(1)} %collective-permute-done.2.refs_9_), channel_id=1, source_target_pairs={{0,1},{1,0},{2,3},{3,2},{4,5},{5,4},{6,7},{7,6},{8,9},{9,8},{10,11... | collective-permute-start | bytes 1572872 | tf_op jit(solution)/shard_map/ppermute | solution.py:203
  30.9 11.2 %collective-permute-start.5 = (bf16[1024,256]{1,0:T(8,128)(2,1)}, bf16[1024,256]{1,0:T(8,128)(2,1)}, u32[]{:S(2)}, u32[]{:S(2)}) collective-permute-start(bf16[1024,256]{1,0:T(8,128)(2,1)} %collective-permute-done.3.refs_10_), channel_id=1, source_target_pairs={{0,4},{1,3},{4,8},{5,1},{8,12},{9,5},{12,14},{13,9},{14,10},{15,13... | collective-permute-start | bytes 1572872 | tf_op jit(solution)/shard_map/ppermute | solution.py:200
  36.5 15.8 %collective-permute-start.7 = (bf16[1024,256]{1,0:T(8,128)(2,1)}, bf16[1024,256]{1,0:T(8,128)(2,1)}, u32[]{:S(2)}, u32[]{:S(2)}) collective-permute-start(bf16[1024,256]{1,0:T(8,128)(2,1)} %collective-permute-done.6.refs_13_), channel_id=1, source_target_pairs={{0,4},{1,3},{4,8},{5,1},{8,12},{9,5},{12,14},{13,9},{14,10},{15,13... | collective-permute-start | bytes 1572872 | tf_op jit(solution)/shard_map/ppermute | solution.py:200
  40.0 18.4 %collective-permute-start.12 = (bf16[1024,256]{1,0:T(8,128)(2,1)}, bf16[1024,256]{1,0:T(8,128)(2,1)}, u32[]{:S(2)}, u32[]{:S(2)}) collective-permute-start(bf16[1024,256]{1,0:T(8,128)(2,1)} %collective-permute-done.3.refs_10_), channel_id=1, source_target_pairs={{0,1},{1,0},{2,3},{3,2},{4,5},{5,4},{6,7},{7,6},{8,9},{9,8},{10,11... | collective-permute-start | bytes 1572872 | tf_op jit(solution)/shard_map/ppermute | solution.py:203
  40.0 0.8 copy-start.2
  40.8 17.6 %collective-permute-start.11 = (bf16[1024,256]{1,0:T(8,128)(2,1)}, bf16[1024,256]{1,0:T(8,128)(2,1)}, u32[]{:S(2)}, u32[]{:S(2)}) collective-permute-start(bf16[1024,256]{1,0:T(8,128)(2,1)} %collective-permute-done.4.refs_11_), channel_id=1, source_target_pairs={{0,1},{1,0},{2,3},{3,2},{4,5},{5,4},{6,7},{7,6},{8,9},{9,8},{10,11... | collective-permute-start | bytes 1572872 | tf_op jit(solution)/shard_map/ppermute | solution.py:203
  42.2 23.1 %collective-permute-start.10 = (bf16[1024,256]{1,0:T(8,128)(2,1)}, bf16[1024,256]{1,0:T(8,128)(2,1)}, u32[]{:S(2)}, u32[]{:S(2)}) collective-permute-start(bf16[1024,256]{1,0:T(8,128)(2,1)} %collective-permute-done.5.refs_12_), channel_id=1, source_target_pairs={{0,1},{1,0},{2,3},{3,2},{4,5},{5,4},{6,7},{7,6},{8,9},{9,8},{10,11... | collective-permute-start | bytes 1572872 | tf_op jit(solution)/shard_map/ppermute | solution.py:203
  42.2 0.8 copy-start.4
  43.0 22.3 %collective-permute-start.9 = (bf16[1024,256]{1,0:T(8,128)(2,1)}, bf16[1024,256]{1,0:T(8,128)(2,1)}, u32[]{:S(2)}, u32[]{:S(2)}) collective-permute-start(bf16[1024,256]{1,0:T(8,128)(2,1)} %collective-permute-done.6.refs_13_), channel_id=1, source_target_pairs={{0,1},{1,0},{2,3},{3,2},{4,5},{5,4},{6,7},{7,6},{8,9},{9,8},{10,11... | collective-permute-start | bytes 1572872 | tf_op jit(solution)/shard_map/ppermute | solution.py:203
  45.9 7.9 %copy-start.1 = (bf16[1024,256]{1,0:T(8,128)(2,1)S(1)}, bf16[1024,256]{1,0:T(8,128)(2,1)}, u32[]{:S(2)}) copy-start(bf16[1024,256]{1,0:T(8,128)(2,1)} %refs_6_.7) | copy-start | bytes 1572868
  52.3 1.5 %copy-start.3 = (bf16[1024,256]{1,0:T(8,128)(2,1)S(1)}, bf16[1024,256]{1,0:T(8,128)(2,1)}, u32[]{:S(2)}) copy-start(bf16[1024,256]{1,0:T(8,128)(2,1)} %copy-done.2) | copy-start | bytes 1572868
  52.3 1.5 %copy-start.5 = (bf16[1024,256]{1,0:T(8,128)(2,1)S(1)}, bf16[1024,256]{1,0:T(8,128)(2,1)}, u32[]{:S(2)}) copy-start(bf16[1024,256]{1,0:T(8,128)(2,1)} %copy-done.4) | copy-start | bytes 1572868
  52.3 1.5 %copy-start.6 = (bf16[96,512]{1,0:T(8,128)(2,1)S(1)}, bf16[96,512]{1,0:T(8,128)(2,1)}, u32[]{:S(2)}) copy-start(bf16[96,512]{1,0:T(8,128)(2,1)} %gather_fusion) | copy-start | bytes 294916
  52.3 1.5 %copy-start.7 = (f32[96,1]{1,0:T(8,128)S(1)}, f32[96,1]{1,0:T(8,128)}, u32[]{:S(2)}) copy-start(f32[96,1]{1,0:T(8,128)} %copy.44.refs_4_) | copy-start | bytes 1156
  52.3 21.4 %collective-permute-start.8 = (bf16[1024,256]{1,0:T(8,128)(2,1)}, bf16[1024,256]{1,0:T(8,128)(2,1)S(1)}, u32[]{:S(2)}, u32[]{:S(2)}) collective-permute-start(bf16[1024,256]{1,0:T(8,128)(2,1)} %collective-permute-done.7.refs_15_), channel_id=1, source_target_pairs={{0,1},{1,0},{2,3},{3,2},{4,5},{5,4},{6,7},{7,6},{8,9},{9,8},{10,11... | collective-permute-start | bytes 1572872 | tf_op jit(solution)/shard_map/ppermute | solution.py:203
  77.6 2.9 %collective-permute-start.15 = (bf16[48,4096]{1,0:T(8,128)(2,1)S(1)}, bf16[48,4096]{1,0:T(8,128)(2,1)S(1)}, u32[]{:S(2)}, u32[]{:S(2)}) collective-permute-start(bf16[48,4096]{1,0:T(8,128)(2,1)S(1)} %get-tuple-element.20), channel_id=1, source_target_pairs={{0,1},{1,0},{2,3},{3,2},{4,5},{5,4},{6,7},{7,6},{8,9},{9,8},{10,11... | collective-permute-start | bytes 1179656 | tf_op jit(solution)/shard_map/ppermute | solution.py:203
